TPU v7x, 32 devices: a whole 2x2x4 slice. The times are simulated.
32 devices in a mesh: parts: 2 (over y), col: 4 (over z), row: 4 (over x, core).
Axes of the slice: x: 2, y: 2, z: 4, core: 2. Of those that a mesh axis runs over, the one named last changes fastest.
Arguments:
- x_tiles: bfloat16 [8, 4, 8, 128, 128], P(('parts', 'row'), 'col'), parts along dimension 0, may hold values from -1.796875 to 1.796875
- x_index: int32 [8, 4, 2, 8], P(('parts', 'row'), 'col'), parts along dimension 0, may hold values from -1 to 3, as said below
- square_index: int32 [8, 4, 2, 8], P(('parts', 'row'), 'col'), parts along dimension 0, may hold values from -1 to 3, as said below
- new_index: int32 [8, 4, 2, 8], P(('parts', 'row'), 'col'), parts along dimension 0, may hold values from -1 to 3, as said below
Outputs:
- squared: bfloat16 [8, 4, 8, 128, 128], P(('parts', 'row'), 'col'), parts along dimension 0
- refined: bfloat16 [8, 4, 8, 128, 128], P(('parts', 'row'), 'col'), parts along dimension 0
There are 2 independent parts, one for each index of `parts`. A program takes and returns all parts, laid end to end along the dimension named above; each array names one. Nothing has to cross between parts.
Inputs may be any that keep to these rules, and one draw needn't show every extreme that they name: `x_index`: entry [r, c, 0, s] is the tile row (0 to 3) and [r, c, 1, s] the tile column (0 to 3) of slot s inside block (r, c); both are -1 for an empty slot, and the filled slots of a block come first and name distinct tiles. No tile row has more than 2 tiles in one block, and some row has exactly 2; some block fills all 8 slots. `square_index`: same layout as x_index. Every named tile (i, j) has some k with tiles (i, k) and (k, j) in X's pattern; no tile row has more than 2 tiles in one block; filled slots name distinct tiles, empty ones are -1 in both entries. `new_index`: same layout as x_index. Every named tile (i, j) has some k with tile (i, k) in X's pattern and (k, j) in square_index; no tile row has more than 2 tiles in one block; filled slots name distinct tiles, empty ones are -1 in both entries.
All inputs are finite; a program needn't handle non-finite values.
Results may differ from a plain program's by a relative error of at most 0.0051.
Values may be sent and summed in bfloat16 or wider, within the bound.
A program may use at most 64 MiB of HBM per device.

v0:
```python
import jax
import jax.numpy as jnp
from jax import lax
from jax.sharding import PartitionSpec as P

ROW_MOST = 2
BLOCK_COLS = 4


def from_behind(block, axis, distance):
    devices = range(lax.axis_size(axis))
    route = [((i - distance) % len(devices), i) for i in devices]
    return lax.ppermute(block, axis, route)


def block_step(running, a_tiles, a_index, k_block, b_tiles, b_row, b_col, target):
    slot_count = a_tiles.shape[0]
    panel_count = b_row.shape[0]
    a_row = a_index[0]
    a_col = a_index[1]
    a_live = a_row >= 0
    slot_ids = jnp.arange(slot_count, dtype=jnp.int32)
    same_row = (
        (a_row[:, None] == a_row[None, :])
        & a_live[None, :]
        & (slot_ids[None, :] < slot_ids[:, None])
    )
    a_rank = jnp.sum(same_row.astype(jnp.int32), axis=1)
    c_row = target[0]
    c_col = target[1]
    rank_ids = jnp.arange(ROW_MOST, dtype=jnp.int32)
    chosen = (a_row[None, None, :] == c_row[:, None, None]) & a_live[None, None, :]
    chosen = (
        chosen & (a_rank[None, None, :] == rank_ids[None, :, None]) & (c_row[:, None, None] >= 0)
    )
    chosen_int = chosen.astype(jnp.int32)
    a_found = jnp.sum(chosen_int, axis=2) > 0
    a_pick = jnp.sum(chosen_int * slot_ids[None, None, :], axis=2) + jnp.where(
        a_found, 0, slot_count
    ).astype(jnp.int32)
    k_row = k_block * BLOCK_COLS + jnp.sum(chosen_int * a_col[None, None, :], axis=2)
    panel_ids = jnp.arange(panel_count, dtype=jnp.int32)
    matched = (
        (b_row[None, None, :] == k_row[:, :, None])
        & (b_col[None, None, :] == c_col[:, None, None])
        & a_found[:, :, None]
    )
    matched_int = matched.astype(jnp.int32)
    b_found = jnp.sum(matched_int, axis=2) > 0
    b_pick = jnp.sum(matched_int * panel_ids[None, None, :], axis=2) + jnp.where(
        b_found, 0, panel_count
    ).astype(jnp.int32)
    padded = jnp.concatenate([a_tiles, jnp.zeros((1,) + a_tiles.shape[1:], a_tiles.dtype)], axis=0)
    left_tiles = padded[a_pick]
    right_tiles = b_tiles[b_pick]
    return running + jnp.einsum(
        "cmij,cmjk->cik", left_tiles, right_tiles, preferred_element_type=jnp.float32
    )


def prepare_panel(panel_tiles, panel_index, row_tiles):
    block_ids = jnp.arange(panel_tiles.shape[0], dtype=jnp.int32)
    raw_rows = panel_index[:, 0, :]
    b_row = jnp.where(raw_rows >= 0, block_ids[:, None] * row_tiles + raw_rows, -1).reshape(-1)
    b_col = panel_index[:, 1, :].reshape(-1)
    flat_tiles = panel_tiles.reshape((-1,) + panel_tiles.shape[2:])
    padded = jnp.concatenate(
        [flat_tiles, jnp.zeros((1,) + flat_tiles.shape[1:], flat_tiles.dtype)], axis=0
    )
    return (padded, b_row, b_col)


def gather_panel(block_tiles, block_index, row_tiles):
    all_tiles, all_index = (
        lax.all_gather(block_tiles, "row", axis=0, tiled=True),
        lax.all_gather(block_index, "row", axis=0, tiled=True),
    )
    return prepare_panel(all_tiles[:, 0], all_index[:, 0], row_tiles)


def circulate(own_tiles, own_index, panel_set, target, col_count, col_here):
    padded, b_row, b_col = panel_set
    depth_count = 1

    def absorb(carried, moving_tiles, moving_index, k_block):
        running, kept_tiles, kept_index = carried
        running = block_step(
            running, moving_tiles, moving_index, k_block, padded, b_row, b_col, target
        )
        return (running, kept_tiles, kept_index)

    carried = (
        jnp.zeros(own_tiles.shape, jnp.float32),
        jnp.zeros((depth_count,) + own_tiles.shape, own_tiles.dtype),
        jnp.zeros((depth_count,) + own_index.shape, jnp.int32),
    )

    def single(turn_no, bundle):
        inner, moving_tiles, moving_index = bundle
        inner = absorb(
            inner, moving_tiles, moving_index, (col_here - turn_no + col_count) % col_count
        )
        moving_tiles, moving_index = from_behind((moving_tiles, moving_index), "col", 1)
        return (inner, moving_tiles, moving_index)

    carried, moving_tiles, moving_index = lax.fori_loop(
        0, col_count - 1, single, (carried, own_tiles, own_index)
    )
    carried = absorb(carried, moving_tiles, moving_index, (col_here + 1) % col_count)
    return (carried[0], (carried[1], carried[2]))


def pick_own(own_tiles, own_index, target):
    slot_count = own_tiles.shape[0]
    slot_ids = jnp.arange(slot_count, dtype=jnp.int32)
    matched = (
        (own_index[0][None, :] == target[0][:, None])
        & (own_index[1][None, :] == target[1][:, None])
        & (own_index[0][None, :] >= 0)
    )
    matched_int = matched.astype(jnp.int32)
    found = jnp.sum(matched_int, axis=1) > 0
    picked = jnp.sum(matched_int * slot_ids[None, :], axis=1) + jnp.where(
        found, 0, slot_count
    ).astype(jnp.int32)
    padded = jnp.concatenate(
        [own_tiles, jnp.zeros((1,) + own_tiles.shape[1:], own_tiles.dtype)], axis=0
    )
    return padded[picked]


def shards(x_tiles, x_index, square_index, new_index):
    col_count = lax.axis_size("col")
    col_here = lax.axis_index("col")
    row_tiles = BLOCK_COLS * col_count // lax.axis_size("row")
    own_tiles = x_tiles[0, 0]
    own_index = x_index[0, 0]
    first_panel = gather_panel(x_tiles, x_index, row_tiles)
    square_sum, history = circulate(
        own_tiles, own_index, first_panel, square_index[0, 0], col_count, col_here
    )
    squared = square_sum.astype(jnp.bfloat16)
    second_panel = gather_panel(squared[None, None], square_index, row_tiles)
    refined_sum, unused = circulate(
        own_tiles, own_index, second_panel, new_index[0, 0], col_count, col_here
    )
    own_part = pick_own(own_tiles, own_index, new_index[0, 0])
    refined = (1.5 * own_part.astype(jnp.float32) - 0.5 * refined_sum).astype(jnp.bfloat16)
    return (squared[None, None], refined[None, None])


def solution(mesh):
    return jax.shard_map(
        shards,
        mesh=mesh,
        in_specs=(
            P(("parts", "row"), "col", None, None, None),
            P(("parts", "row"), "col", None, None),
            P(("parts", "row"), "col", None, None),
            P(("parts", "row"), "col", None, None),
        ),
        out_specs=(
            P(("parts", "row"), "col", None, None, None),
            P(("parts", "row"), "col", None, None, None),
        ),
        check_vma=False,
    )
```

profile of v0, /device:TPU:0, one launch (start us, length us, event | category | flops | bytes accessed | tf_op | source)
XLA Modules:
  0.0 119.9 jit_solution(961044786944197622)
XLA Ops:
  7.2 1.7 %copy.98 = bf16[1,1,8,128,128]{4,3,2,1,0:T(8,128)(2,1)} copy(bf16[1,1,8,128,128]{4,3,2,1,0:T(8,128)(2,1)} %param.8) | data formatting | bytes 524288
  8.9 0.7 copy.99
  9.7 6.3 %all_gather.14 = s32[4,1,2,8]{3,2,1,0:T(2,128)S(1)} all-gather(s32[1,1,2,8]{3,2,1,0:T(2,128)} %param.10), channel_id=1, replica_groups=mesh['parts'=2,'col'=4,'row'=4] {'row'}, dimensions={0}, use_global_device_ids=true | all-gather | bytes 320 | tf_op jit(solution)/shard_map/all_gather | solution.py:76
  15.9 5.3 %all_gather.12 = s32[4,1,2,8]{3,2,1,0:T(2,128)S(1)} all-gather(s32[1,1,2,8]{3,2,1,0:T(2,128)S(1)} %copy.99), channel_id=1, replica_groups=mesh['parts'=2,'col'=4,'row'=4] {'row'}, dimensions={0}, use_global_device_ids=true | all-gather | bytes 320 | tf_op jit(solution)/shard_map/all_gather | solution.py:76
  21.5 1.0 copy.76
  23.0 6.6 %all-gather.4.cloned.1.call-done = bf16[4,1,8,128,128]{4,3,2,1,0:T(8,128)(2,1)} async-done(((bf16[1,1,8,128,128]{4,3,2,1,0:T(8,128)(2,1)}), bf16[4,1,8,128,128]{4,3,2,1,0:T(8,128)(2,1)}) %all-gather.4.cloned.1.call-update) | async-done | bytes 1048592 | tf_op jit(solution)/shard_map/all_gather | solution.py:75
  29.6 1.3 %concatenate.25 = bf16[33,128,128]{2,1,0:T(8,128)(2,1)S(1)} pad(bf16[32,128,128]{2,1,0:T(8,128)(2,1)} %bitcast.241, bf16[]{:T(256)} %constant.256.clone.1), padding=0_1x0_0x0_0 | pad | bytes 2129922 | tf_op jit(solution)/shard_map/concatenate | solution.py:67
  30.9 29.1 %while.42 = (s32[]{:T(128)}, f32[8,128,128]{2,1,0:T(8,128)S(1)}, bf16[8,128,128]{2,1,0:T(8,128)(2,1)S(1)}, s32[2,8]{1,0:T(2,128)S(1)}, s32[2,8]{1,0:T(2,128)S(1)...) while((s32[]{:T(128)}, f32[8,128,128]{2,1,0:T(8,128)S(1)}, ...), condition=%wide.wide.region_7.8_spmd.clone, body=%wide.wide.region_0.7_spmd.clone.sunk | while | flops 67378608 | bytes 6336438 | solution.py:106
  31.0 1.5 %collective-permute-start.1 = (s32[2,8]{1,0:T(2,128)S(1)}, s32[2,8]{1,0:T(2,128)S(1)}, u32[]{:S(2)}, u32[]{:S(2)}) collective-permute-start(s32[2,8]{1,0:T(2,128)S(1)} %copy.81), channel_id=1, source_target_pairs={{12,0},{0,4},{4,8},{8,12},{13,1},{1,5},{5,9},{9,13},{14,2},{2,6},{... | collective-permute-start | bytes 200 | tf_op jit(solution)/shard_map/while/body/eval_jaxpr/ppermute | solution.py:13
  32.5 1.5 %collective-permute-start = (bf16[8,128,128]{2,1,0:T(8,128)(2,1)S(1)}, bf16[8,128,128]{2,1,0:T(8,128)(2,1)S(1)}, u32[]{:S(2)}, u32[]{:S(2)}) collective-permute-start(bf16[8,128,128]{2,1,0:T(8,128)(2,1)S(1)} %copy.80), channel_id=1, source_target_pairs={{12,0},{0,4},{4,8},{8,12},{13,1},{1,5},{5,9},{9,13},{14,2},{2,6},{... | collective-permute-start | bytes 786440 | tf_op jit(solution)/shard_map/while/body/eval_jaxpr/ppermute | solution.py:13
  35.4 0.7 gather_fusion
  37.1 5.5 %collective-permute-done = bf16[8,128,128]{2,1,0:T(8,128)(2,1)S(1)} collective-permute-done((bf16[8,128,128]{2,1,0:T(8,128)(2,1)S(1)}, bf16[8,128,128]{2,1,0:T(8,128)(2,1)S(1)}, u32[]{:S(2)}, u32[]{:S(2)}) %collective-permute-start) | collective-permute-done | bytes 262176 | tf_op jit(solution)/shard_map/while/body/eval_jaxpr/ppermute | solution.py:13
  42.6 1.2 %collective-permute-start = (bf16[8,128,128]{2,1,0:T(8,128)(2,1)S(1)}, bf16[8,128,128]{2,1,0:T(8,128)(2,1)S(1)}, u32[]{:S(2)}, u32[]{:S(2)}) collective-permute-start(bf16[8,128,128]{2,1,0:T(8,128)(2,1)S(1)} %copy.80), channel_id=1, source_target_pairs={{12,0},{0,4},{4,8},{8,12},{13,1},{1,5},{5,9},{9,13},{14,2},{2,6},{... | collective-permute-start | bytes 786440 | tf_op jit(solution)/shard_map/while/body/eval_jaxpr/ppermute | solution.py:13
  45.1 0.7 gather_fusion
  46.8 1.2 collective-permute-done.1
  48.0 3.8 %collective-permute-done = bf16[8,128,128]{2,1,0:T(8,128)(2,1)S(1)} collective-permute-done((bf16[8,128,128]{2,1,0:T(8,128)(2,1)S(1)}, bf16[8,128,128]{2,1,0:T(8,128)(2,1)S(1)}, u32[]{:S(2)}, u32[]{:S(2)}) %collective-permute-start) | collective-permute-done | bytes 262176 | tf_op jit(solution)/shard_map/while/body/eval_jaxpr/ppermute | solution.py:13
  55.2 2.0 %collective-permute-done.1 = s32[2,8]{1,0:T(2,128)S(1)} collective-permute-done((s32[2,8]{1,0:T(2,128)S(1)}, s32[2,8]{1,0:T(2,128)S(1)}, u32[]{:S(2)}, u32[]{:S(2)}) %collective-permute-start.1) | collective-permute-done | bytes 96 | tf_op jit(solution)/shard_map/while/body/eval_jaxpr/ppermute | solution.py:13
  57.2 2.9 %collective-permute-done = bf16[8,128,128]{2,1,0:T(8,128)(2,1)S(1)} collective-permute-done((bf16[8,128,128]{2,1,0:T(8,128)(2,1)S(1)}, bf16[8,128,128]{2,1,0:T(8,128)(2,1)S(1)}, u32[]{:S(2)}, u32[]{:S(2)}) %collective-permute-start) | collective-permute-done | bytes 262176 | tf_op jit(solution)/shard_map/while/body/eval_jaxpr/ppermute | solution.py:13
  62.6 1.0 fusion.13
  64.2 1.3 %gather_fusion.6 = bf16[8,128,128]{2,1,0:T(8,128)(2,1)} fusion(bf16[9,128,128]{2,1,0:T(8,128)(2,1)S(1)} %concatenate.27, s32[1024]{0:T(1024)S(1)} %pad_clamp_fusion.6), kind=kCustom, calls=%fused_computation.6 | custom fusion | bytes 524320 | tf_op jit(solution)/shard_map/gather | solution.py:129
  65.6 13.5 %all-gather.6.cloned.1.call-done = bf16[32,128,128]{2,1,0:T(8,128)(2,1)} async-done(((bf16[8,128,128]{2,1,0:T(8,128)(2,1)}), bf16[32,128,128]{2,1,0:T(8,128)(2,1)}) %all-gather.6.cloned.1.call-update) | async-done | bytes 1048592 | tf_op jit(solution)/shard_map/all_gather | solution.py:75
  79.1 1.3 %concatenate.28 = bf16[33,128,128]{2,1,0:T(8,128)(2,1)S(1)} pad(bf16[32,128,128]{2,1,0:T(8,128)(2,1)} %all-gather.6.cloned.1.call-done, bf16[]{:T(256)} %constant.256.clone.1), padding=0_1x0_0x0_0 | pad | bytes 2129922 | tf_op jit(solution)/shard_map/concatenate | solution.py:67
  80.4 29.1 %while.43 = (s32[]{:T(128)}, f32[8,128,128]{2,1,0:T(8,128)S(1)}, bf16[8,128,128]{2,1,0:T(8,128)(2,1)S(1)}, s32[2,8]{1,0:T(2,128)S(1)}, s32[2,8]{1,0:T(2,128)S(1)...) while((s32[]{:T(128)}, f32[8,128,128]{2,1,0:T(8,128)S(1)}, ...), condition=%wide.wide.region_23.24_spmd.clone, body=%wide.wide.region_16.23_spmd.clone.sunk | while | flops 67378608 | bytes 6336438 | solution.py:106
  80.5 1.5 %collective-permute-start.3 = (s32[2,8]{1,0:T(2,128)S(1)}, s32[2,8]{1,0:T(2,128)S(1)}, u32[]{:S(2)}, u32[]{:S(2)}) collective-permute-start(s32[2,8]{1,0:T(2,128)S(1)} %copy.93), channel_id=1, source_target_pairs={{12,0},{0,4},{4,8},{8,12},{13,1},{1,5},{5,9},{9,13},{14,2},{2,6},{... | collective-permute-start | bytes 200 | tf_op jit(solution)/shard_map/while/body/eval_jaxpr/ppermute | solution.py:13
  82.0 1.5 %collective-permute-start.2 = (bf16[8,128,128]{2,1,0:T(8,128)(2,1)S(1)}, bf16[8,128,128]{2,1,0:T(8,128)(2,1)S(1)}, u32[]{:S(2)}, u32[]{:S(2)}) collective-permute-start(bf16[8,128,128]{2,1,0:T(8,128)(2,1)S(1)} %copy.92), channel_id=1, source_target_pairs={{12,0},{0,4},{4,8},{8,12},{13,1},{1,5},{5,9},{9,13},{14,2},{2,6},{... | collective-permute-start | bytes 786440 | tf_op jit(solution)/shard_map/while/body/eval_jaxpr/ppermute | solution.py:13
  86.6 5.5 %collective-permute-done.2 = bf16[8,128,128]{2,1,0:T(8,128)(2,1)S(1)} collective-permute-done((bf16[8,128,128]{2,1,0:T(8,128)(2,1)S(1)}, bf16[8,128,128]{2,1,0:T(8,128)(2,1)S(1)}, u32[]{:S(2)}, u32[]{:S(2)}) %collective-permute-start.2) | collective-permute-done | bytes 262176 | tf_op jit(solution)/shard_map/while/body/eval_jaxpr/ppermute | solution.py:13
  92.1 1.2 %collective-permute-start.2 = (bf16[8,128,128]{2,1,0:T(8,128)(2,1)S(1)}, bf16[8,128,128]{2,1,0:T(8,128)(2,1)S(1)}, u32[]{:S(2)}, u32[]{:S(2)}) collective-permute-start(bf16[8,128,128]{2,1,0:T(8,128)(2,1)S(1)} %copy.92), channel_id=1, source_target_pairs={{12,0},{0,4},{4,8},{8,12},{13,1},{1,5},{5,9},{9,13},{14,2},{2,6},{... | collective-permute-start | bytes 786440 | tf_op jit(solution)/shard_map/while/body/eval_jaxpr/ppermute | solution.py:13
  96.3 1.2 collective-permute-done.3
  97.5 3.8 %collective-permute-done.2 = bf16[8,128,128]{2,1,0:T(8,128)(2,1)S(1)} collective-permute-done((bf16[8,128,128]{2,1,0:T(8,128)(2,1)S(1)}, bf16[8,128,128]{2,1,0:T(8,128)(2,1)S(1)}, u32[]{:S(2)}, u32[]{:S(2)}) %collective-permute-start.2) | collective-permute-done | bytes 262176 | tf_op jit(solution)/shard_map/while/body/eval_jaxpr/ppermute | solution.py:13
  104.7 2.0 %collective-permute-done.3 = s32[2,8]{1,0:T(2,128)S(1)} collective-permute-done((s32[2,8]{1,0:T(2,128)S(1)}, s32[2,8]{1,0:T(2,128)S(1)}, u32[]{:S(2)}, u32[]{:S(2)}) %collective-permute-start.3) | collective-permute-done | bytes 96 | tf_op jit(solution)/shard_map/while/body/eval_jaxpr/ppermute | solution.py:13
  106.7 2.9 %collective-permute-done.2 = bf16[8,128,128]{2,1,0:T(8,128)(2,1)S(1)} collective-permute-done((bf16[8,128,128]{2,1,0:T(8,128)(2,1)S(1)}, bf16[8,128,128]{2,1,0:T(8,128)(2,1)S(1)}, u32[]{:S(2)}, u32[]{:S(2)}) %collective-permute-start.2) | collective-permute-done | bytes 262176 | tf_op jit(solution)/shard_map/while/body/eval_jaxpr/ppermute | solution.py:13
  112.1 1.0 fusion.14
  (239 shorter events, 23.5 us)
Async XLA Ops:
  7.2 15.7 %copy-start.2 = (s32[1,1,2,8]{3,2,1,0:T(2,128)S(1)}, s32[1,1,2,8]{3,2,1,0:T(2,128)}, u32[]{:S(2)}) copy-start(s32[1,1,2,8]{3,2,1,0:T(2,128)} %param.10) | copy-start | bytes 196
  7.2 22.4 %all-gather.4.cloned.1.call-start = ((), (), s32[]{:S(2)}) async-start(), calls=%async_computation | async-start | bytes 1310720 | tf_op jit(solution)/shard_map/all_gather | solution.py:75
  9.6 69.5 %all-gather.6.cloned.1.call-start = ((), (), s32[]{:S(2)}) async-start(), calls=%async_computation.1 | async-start | bytes 1310720 | tf_op jit(solution)/shard_map/all_gather | solution.py:75
  21.3 9.7 %copy-start.6 = (s32[4,1,8]{2,1,0:T(1,128)}, s32[4,1,8]{2,1,0:T(1,128)S(1)}, u32[]{:S(2)}) copy-start(s32[4,1,8]{2,1,0:T(1,128)S(1)} %get-tuple-element.691) | copy-start | bytes 388
  21.3 42.5 %copy-start.4 = (s32[4,1,8]{2,1,0:T(1,128)}, s32[4,1,8]{2,1,0:T(1,128)S(1)}, u32[]{:S(2)}) copy-start(s32[4,1,8]{2,1,0:T(1,128)S(1)} %get-tuple-element.672) | copy-start | bytes 388
  21.3 9.6 %copy-start.7 = (s32[4,8]{1,0:T(4,128)}, s32[4,8]{1,0:T(4,128)S(1)}, u32[]{:S(2)}) copy-start(s32[4,8]{1,0:T(4,128)S(1)} %get-tuple-element.981) | copy-start | bytes 388
  21.3 42.3 %copy-start.5 = (s32[4,8]{1,0:T(4,128)}, s32[4,8]{1,0:T(4,128)S(1)}, u32[]{:S(2)}) copy-start(s32[4,8]{1,0:T(4,128)S(1)} %get-tuple-element.1029) | copy-start | bytes 388
  31.0 6.1 %collective-permute-start.1 = (s32[2,8]{1,0:T(2,128)S(1)}, s32[2,8]{1,0:T(2,128)S(1)}, u32[]{:S(2)}, u32[]{:S(2)}) collective-permute-start(s32[2,8]{1,0:T(2,128)S(1)} %copy.81), channel_id=1, source_target_pairs={{12,0},{0,4},{4,8},{8,12},{13,1},{1,5},{5,9},{9,13},{14,2},{2,6},{... | collective-permute-start | bytes 200 | tf_op jit(solution)/shard_map/while/body/eval_jaxpr/ppermute | solution.py:13
  32.5 10.0 %collective-permute-start = (bf16[8,128,128]{2,1,0:T(8,128)(2,1)S(1)}, bf16[8,128,128]{2,1,0:T(8,128)(2,1)S(1)}, u32[]{:S(2)}, u32[]{:S(2)}) collective-permute-start(bf16[8,128,128]{2,1,0:T(8,128)(2,1)S(1)} %copy.80), channel_id=1, source_target_pairs={{12,0},{0,4},{4,8},{8,12},{13,1},{1,5},{5,9},{9,13},{14,2},{2,6},{... | collective-permute-start | bytes 786440 | tf_op jit(solution)/shard_map/while/body/eval_jaxpr/ppermute | solution.py:13
  42.5 5.4 %collective-permute-start.1 = (s32[2,8]{1,0:T(2,128)S(1)}, s32[2,8]{1,0:T(2,128)S(1)}, u32[]{:S(2)}, u32[]{:S(2)}) collective-permute-start(s32[2,8]{1,0:T(2,128)S(1)} %copy.81), channel_id=1, source_target_pairs={{12,0},{0,4},{4,8},{8,12},{13,1},{1,5},{5,9},{9,13},{14,2},{2,6},{... | collective-permute-start | bytes 200 | tf_op jit(solution)/shard_map/while/body/eval_jaxpr/ppermute | solution.py:13
  42.6 9.2 %collective-permute-start = (bf16[8,128,128]{2,1,0:T(8,128)(2,1)S(1)}, bf16[8,128,128]{2,1,0:T(8,128)(2,1)S(1)}, u32[]{:S(2)}, u32[]{:S(2)}) collective-permute-start(bf16[8,128,128]{2,1,0:T(8,128)(2,1)S(1)} %copy.80), channel_id=1, source_target_pairs={{12,0},{0,4},{4,8},{8,12},{13,1},{1,5},{5,9},{9,13},{14,2},{2,6},{... | collective-permute-start | bytes 786440 | tf_op jit(solution)/shard_map/while/body/eval_jaxpr/ppermute | solution.py:13
  51.7 5.4 %collective-permute-start.1 = (s32[2,8]{1,0:T(2,128)S(1)}, s32[2,8]{1,0:T(2,128)S(1)}, u32[]{:S(2)}, u32[]{:S(2)}) collective-permute-start(s32[2,8]{1,0:T(2,128)S(1)} %copy.81), channel_id=1, source_target_pairs={{12,0},{0,4},{4,8},{8,12},{13,1},{1,5},{5,9},{9,13},{14,2},{2,6},{... | collective-permute-start | bytes 200 | tf_op jit(solution)/shard_map/while/body/eval_jaxpr/ppermute | solution.py:13
  51.8 8.3 %collective-permute-start = (bf16[8,128,128]{2,1,0:T(8,128)(2,1)S(1)}, bf16[8,128,128]{2,1,0:T(8,128)(2,1)S(1)}, u32[]{:S(2)}, u32[]{:S(2)}) collective-permute-start(bf16[8,128,128]{2,1,0:T(8,128)(2,1)S(1)} %copy.80), channel_id=1, source_target_pairs={{12,0},{0,4},{4,8},{8,12},{13,1},{1,5},{5,9},{9,13},{14,2},{2,6},{... | collective-permute-start | bytes 786440 | tf_op jit(solution)/shard_map/while/body/eval_jaxpr/ppermute | solution.py:13
  62.6 1.1 copy-start
  62.6 1.4 %copy-start.3 = (s32[1,1,2,8]{3,2,1,0:T(2,128)S(1)}, s32[1,1,2,8]{3,2,1,0:T(2,128)}, u32[]{:S(2)}) copy-start(s32[1,1,2,8]{3,2,1,0:T(2,128)} %param.11) | copy-start | bytes 196
  80.5 6.1 %collective-permute-start.3 = (s32[2,8]{1,0:T(2,128)S(1)}, s32[2,8]{1,0:T(2,128)S(1)}, u32[]{:S(2)}, u32[]{:S(2)}) collective-permute-start(s32[2,8]{1,0:T(2,128)S(1)} %copy.93), channel_id=1, source_target_pairs={{12,0},{0,4},{4,8},{8,12},{13,1},{1,5},{5,9},{9,13},{14,2},{2,6},{... | collective-permute-start | bytes 200 | tf_op jit(solution)/shard_map/while/body/eval_jaxpr/ppermute | solution.py:13
  82.0 10.0 %collective-permute-start.2 = (bf16[8,128,128]{2,1,0:T(8,128)(2,1)S(1)}, bf16[8,128,128]{2,1,0:T(8,128)(2,1)S(1)}, u32[]{:S(2)}, u32[]{:S(2)}) collective-permute-start(bf16[8,128,128]{2,1,0:T(8,128)(2,1)S(1)} %copy.92), channel_id=1, source_target_pairs={{12,0},{0,4},{4,8},{8,12},{13,1},{1,5},{5,9},{9,13},{14,2},{2,6},{... | collective-permute-start | bytes 786440 | tf_op jit(solution)/shard_map/while/body/eval_jaxpr/ppermute | solution.py:13
  92.0 5.4 %collective-permute-start.3 = (s32[2,8]{1,0:T(2,128)S(1)}, s32[2,8]{1,0:T(2,128)S(1)}, u32[]{:S(2)}, u32[]{:S(2)}) collective-permute-start(s32[2,8]{1,0:T(2,128)S(1)} %copy.93), channel_id=1, source_target_pairs={{12,0},{0,4},{4,8},{8,12},{13,1},{1,5},{5,9},{9,13},{14,2},{2,6},{... | collective-permute-start | bytes 200 | tf_op jit(solution)/shard_map/while/body/eval_jaxpr/ppermute | solution.py:13
  92.1 9.2 %collective-permute-start.2 = (bf16[8,128,128]{2,1,0:T(8,128)(2,1)S(1)}, bf16[8,128,128]{2,1,0:T(8,128)(2,1)S(1)}, u32[]{:S(2)}, u32[]{:S(2)}) collective-permute-start(bf16[8,128,128]{2,1,0:T(8,128)(2,1)S(1)} %copy.92), channel_id=1, source_target_pairs={{12,0},{0,4},{4,8},{8,12},{13,1},{1,5},{5,9},{9,13},{14,2},{2,6},{... | collective-permute-start | bytes 786440 | tf_op jit(solution)/shard_map/while/body/eval_jaxpr/ppermute | solution.py:13
  101.2 5.4 %collective-permute-start.3 = (s32[2,8]{1,0:T(2,128)S(1)}, s32[2,8]{1,0:T(2,128)S(1)}, u32[]{:S(2)}, u32[]{:S(2)}) collective-permute-start(s32[2,8]{1,0:T(2,128)S(1)} %copy.93), channel_id=1, source_target_pairs={{12,0},{0,4},{4,8},{8,12},{13,1},{1,5},{5,9},{9,13},{14,2},{2,6},{... | collective-permute-start | bytes 200 | tf_op jit(solution)/shard_map/while/body/eval_jaxpr/ppermute | solution.py:13
  101.3 8.3 %collective-permute-start.2 = (bf16[8,128,128]{2,1,0:T(8,128)(2,1)S(1)}, bf16[8,128,128]{2,1,0:T(8,128)(2,1)S(1)}, u32[]{:S(2)}, u32[]{:S(2)}) collective-permute-start(bf16[8,128,128]{2,1,0:T(8,128)(2,1)S(1)} %copy.92), channel_id=1, source_target_pairs={{12,0},{0,4},{4,8},{8,12},{13,1},{1,5},{5,9},{9,13},{14,2},{2,6},{... | collective-permute-start | bytes 786440 | tf_op jit(solution)/shard_map/while/body/eval_jaxpr/ppermute | solution.py:13
  110.5 1.5 %copy-start.1 = (bf16[8,128,128]{2,1,0:T(8,128)(2,1)S(1)}, bf16[8,128,128]{2,1,0:T(8,128)(2,1)}, u32[]{:S(2)}) copy-start(bf16[8,128,128]{2,1,0:T(8,128)(2,1)} %gather_fusion.6) | copy-start | bytes 786436
Sparse Core Ops, SparseCore 0:
  10.1 19.4 all-gather.3
  63.7 15.3 all-gather.5
where the time goes:
time: 120 us
  waiting for transfers between devices  50.7 us (42%)
  local copies, waits for them, and re-layouts  21.5 us (18%)
  between operations  14.4 us (12%)
  blocking collectives  11.5 us (10%)
  starting transfers between devices  9.53 us (8%)
  other arithmetic  7.19 us (6%)
  matrix products  4.37 us (4%)
    ppermute x12, waiting for transfers between devices, from_behind(): return lax.ppermute(block, axis, route)  30.5 us
    all_gather x2, waiting for transfers between devices, gather_panel(): lax.all_gather(block_tiles, 'row', axis=0, tiled=True)  20.2 us
    all_gather x2, blocking collectives, gather_panel(): lax.all_gather(block_index, 'row', axis=0, tiled=True)  11.5 us
    ppermute x12, starting transfers between devices, from_behind(): return lax.ppermute(block, axis, route)  9.45 us
    gather x8, local copies, waits for them, and re-layouts, block_step(): left_tiles = padded[a_pick]  5.21 us
    gather x8, local copies, waits for them, and re-layouts, block_step(): right_tiles = b_tiles[b_pick]  5.19 us
    dot_general x8, matrix products, block_step(): jnp.einsum('cmij,cmjk->cik', left_tiles, right_tiles, preferred_element_t...  4.37 us
    unnamed x20, local copies, waits for them, and re-layouts  3.35 us
  transfers between devices with their start and end apart: 14, of which 12 were waited for; matrix products, arithmetic and copies ran while one was open for 18% of the time, Pallas kernels for 0%

commit v1 on v0

v1 whole, which is shorter than its diff:
```python
import functools

import jax
import jax.numpy as jnp
from jax import lax
from jax.experimental import pallas as pl
from jax.experimental.pallas import tpu as pltpu
from jax.sharding import PartitionSpec as P

MESH = pl.DeviceIdType.MESH
ROW_MOST = 2
BLOCK_COLS = 4
META = 16
FEW = 8
BF16 = jnp.bfloat16
F32 = jnp.float32


def loop(count, body):
    if count <= FEW:
        for i in range(count):
            body(i)
    else:
        lax.fori_loop(0, count, lambda i, _: (body(i), 0)[1], 0)


class Plan:
    def __init__(self, n_col, n_row, slots, tile, chunks):
        self.n_col, self.n_row, self.slots, self.tile = n_col, n_row, slots, tile
        self.rows = BLOCK_COLS * n_col // n_row
        self.canonical = self.rows * ROW_MOST <= slots
        self.chunks = chunks if self.canonical and self.rows % chunks == 0 else 1
        self.pos = self.rows * ROW_MOST if self.canonical else slots
        self.rc = self.rows // self.chunks
        self.pc = self.pos // self.chunks
        self.ch = self.pc * tile + META
        self.places = self.rows * BLOCK_COLS
        self.small = self.rows <= FEW and n_col <= FEW
        self.width = BLOCK_COLS * tile
        assert self.pc <= META and self.places <= 256 and n_row % 2 == 0


def slot_keys(plan, idx):
    rows = [idx[0, 0, 0, s] for s in range(plan.slots)]
    out = []
    if not plan.canonical:
        for s in range(plan.slots):
            out.append((s, jnp.where(rows[s] >= 0, rows[s] * BLOCK_COLS + idx[0, 0, 1, s], -1)))
        return out
    for i in range(plan.rows):
        found = [jnp.int32(plan.slots)] * ROW_MOST
        for s in reversed(range(plan.slots)):
            hit = rows[s] == i
            found = [
                jnp.where(hit, found[k - 1] if k else jnp.int32(s), found[k]) for k in range(ROW_MOST)
            ]
        for slot in found:
            live = slot < plan.slots
            slot = jnp.minimum(slot, plan.slots - 1)
            out.append((slot, jnp.where(live, i * BLOCK_COLS + idx[0, 0, 1, slot], -1)))
    return out


def out_keys(plan, idx):
    rows = [idx[0, 0, 0, s] for s in range(plan.slots)]
    return [
        jnp.where(rows[s] >= 0, rows[s] * BLOCK_COLS + idx[0, 0, 1, s], plan.places)
        for s in range(plan.slots)
    ]


def meta_of(plan, keys):
    place = lax.broadcasted_iota(jnp.int32, (META, plan.tile), 0)
    meta = jnp.full((META, plan.tile), -1, jnp.int32)
    for p, key in enumerate(keys):
        meta = jnp.where(place == p, key, meta)
    return meta.astype(F32).astype(BF16)


def row_tiles(plan, chunk, i, il):
    t = plan.tile
    meta = chunk[plan.pc * t : plan.pc * t + META, :].astype(F32)
    cands = range(il * ROW_MOST, (il + 1) * ROW_MOST) if plan.canonical else range(plan.pc)
    out = []
    for j in range(BLOCK_COLS):
        key = jnp.asarray(i * BLOCK_COLS + j, jnp.int32).astype(F32)
        total = None
        for p in cands:
            here = jnp.broadcast_to(meta[p : p + 1, :], (META, t)) == key
            mask = jnp.where(here, 1.0, 0.0).astype(BF16)
            part = chunk[p * t : (p + 1) * t, :].reshape(t // META, META, t) * mask[None]
            total = part if total is None else total + part
        out.append(total.reshape(t, t))
    return out


def kernel(
    plan,
    x_ref, xi_ref, si_ref, ni_ref,
    sq_ref, rf_ref,
    pk, sk, zbuf, rbuf, sbuf, bd, ld, acc, xt, *rest,
):
    if plan.small:
        sd, acc2, *sems = rest
    else:
        sd, acc2, sems = bd, acc, rest
    zrecv, up_send, dn_send, rrecv, pair_send, cross_send, relay_send, srecv, spair_send, scross_send, srelay_send = sems
    n_col, n_row, t, chunks = plan.n_col, plan.n_row, plan.tile, plan.chunks
    c = lax.axis_index("col")
    r = lax.axis_index("row")
    pair = r + 1 - 2 * lax.rem(r, 2)
    hops = range(1, n_row // 2)
    crosses = [lax.rem(r + 2 * m, n_row) for m in hops]
    sources = [lax.rem(r + n_row - 2 * m, n_row) for m in hops]
    relayed = [lax.rem(pair + n_row - 2 * m, n_row) for m in hops]

    barrier = pltpu.get_barrier_semaphore()

    @pl.when(c > 0)
    def _():
        pl.semaphore_signal(barrier, inc=1, device_id={"col": c - 1}, device_id_type=MESH)

    @pl.when(c < n_col - 1)
    def _():
        pl.semaphore_signal(barrier, inc=1, device_id={"col": c + 1}, device_id_type=MESH)

    for other in [pair] + crosses:
        pl.semaphore_signal(barrier, inc=1, device_id={"row": other}, device_id_type=MESH)

    x_keys = slot_keys(plan, xi_ref)
    for g in range(chunks):
        mine = x_keys[g * plan.pc : (g + 1) * plan.pc]
        for p, (slot, _) in enumerate(mine):
            pk[g, p * t : (p + 1) * t, :] = x_ref[0, 0, slot]
        pk[g, plan.pc * t : plan.ch, :] = meta_of(plan, [key for _, key in mine])

    inner = jnp.where(c > 0, 1, 0) + jnp.where(c < n_col - 1, 1, 0)
    pl.semaphore_wait(barrier, inner + 1 + len(crosses))

    def col_copy(src, kb, g, send, to):
        return pltpu.make_async_remote_copy(
            src_ref=src, dst_ref=zbuf.at[kb, g], send_sem=send.at[kb, g], recv_sem=zrecv.at[kb, g],
            device_id={"col": to}, device_id_type=MESH,
        )

    def row_copy(src, dst, origin, g, send, recv, to):
        return pltpu.make_async_remote_copy(
            src_ref=src, dst_ref=dst.at[origin, g], send_sem=send, recv_sem=recv.at[origin, g],
            device_id={"row": to}, device_id_type=MESH,
        )

    def send_row(src, dst, g, pair_sem, cross_sem, recv):
        for m, to in enumerate(crosses):
            row_copy(src.at[g], dst, r, g, cross_sem.at[m, g], recv, to).start()
        row_copy(src.at[g], dst, r, g, pair_sem.at[g], recv, pair).start()

    def take_cross(dst, g, relay_sem, recv):
        for m, origin in enumerate(sources):
            hop = row_copy(dst.at[origin, g], dst, origin, g, relay_sem.at[m, g], recv, pair)
            hop.wait_recv()
            hop.start()

    def take_pair(dst, g, recv, relay_sem):
        row_copy(dst.at[pair, g], dst, pair, g, relay_sem.at[0, g], recv, pair).wait_recv()

    def take_relayed(dst, g, recv, relay_sem):
        for origin in relayed:
            row_copy(dst.at[origin, g], dst, origin, g, relay_sem.at[0, g], recv, pair).wait_recv()

    def end_row(src, dst, g, pair_sem, cross_sem, relay_sem, recv):
        row_copy(src.at[g], dst, r, g, pair_sem.at[g], recv, pair).wait_send()
        for m, to in enumerate(crosses):
            row_copy(src.at[g], dst, r, g, cross_sem.at[m, g], recv, to).wait_send()
        for m, origin in enumerate(sources):
            row_copy(dst.at[origin, g], dst, origin, g, relay_sem.at[m, g], recv, pair).wait_send()

    for g in range(chunks):
        @pl.when(c < n_col - 1)
        def _():
            col_copy(pk.at[g], c, g, up_send, c + 1).start()

        @pl.when(c > 0)
        def _():
            col_copy(pk.at[g], c, g, dn_send, c - 1).start()

        send_row(pk, rbuf, g, pair_send, cross_send, rrecv)

    acc[plan.places] = jnp.zeros((t, t), F32)
    acc2[plan.places] = jnp.zeros((t, t), F32)
    xt[plan.places] = jnp.zeros((t, t), BF16)

    def forward(d, g):
        @pl.when(c >= d)
        def _():
            col_copy(zbuf.at[c - d, g], c - d, g, up_send, c).wait_recv()

            @pl.when(c < n_col - 1)
            def _():
                col_copy(zbuf.at[c - d, g], c - d, g, up_send, c + 1).start()

        @pl.when(c + d < n_col)
        def _():
            col_copy(zbuf.at[c + d, g], c + d, g, dn_send, c).wait_recv()

            @pl.when(c > 0)
            def _():
                col_copy(zbuf.at[c + d, g], c + d, g, dn_send, c - 1).start()

    def unpack(chunk, origin, g, dense):
        def one(il):
            i = g * plan.rc + il
            for j, tile in enumerate(row_tiles(plan, chunk, i, il)):
                dense[origin * plan.rows + i, :, j * t : (j + 1) * t] = tile
        loop(plan.rc, one)

    def right_of(dense, kb):
        return dense[pl.ds(kb * BLOCK_COLS, BLOCK_COLS)].reshape(plan.width, plan.width)

    def add(into, i, product, first):
        for j in range(BLOCK_COLS):
            part = product[:, j * t : (j + 1) * t]
            if first:
                into[i * BLOCK_COLS + j] = part
            else:
                into[i * BLOCK_COLS + j] += part

    def multiply(chunk, kb, g, dense, into, first):
        def one(il):
            i = g * plan.rc + il
            left = jnp.concatenate(row_tiles(plan, chunk, i, il), axis=1)
            add(into, i, jnp.dot(left, right_of(dense, kb), preferred_element_type=F32), first)

        if not plan.small:
            loop(plan.rc, one)
            return
        for il in range(plan.rc):
            for j, tile in enumerate(row_tiles(plan, chunk, g * plan.rc + il, il)):
                ld[kb, g * plan.rc + il, :, j * t : (j + 1) * t] = tile
        left = ld[kb, g * plan.rc : (g + 1) * plan.rc].reshape(plan.rc * t, plan.width)
        product = jnp.dot(left, right_of(dense, kb), preferred_element_type=F32)
        for il in range(plan.rc):
            add(into, g * plan.rc + il, product[il * t : (il + 1) * t], first)

    def multiply_pair(d, g, dense, into):
        @pl.when(c >= d)
        def _():
            multiply(zbuf.at[c - d, g], c - d, g, dense, into, False)

        @pl.when(c + d < n_col)
        def _():
            multiply(zbuf.at[c + d, g], c + d, g, dense, into, False)

    for g in range(chunks):
        take_cross(rbuf, g, relay_send, rrecv)
        forward(1, g)
    for g in range(chunks):
        unpack(pk.at[g], r, g, bd)
        take_pair(rbuf, g, rrecv, relay_send)
        unpack(rbuf.at[pair, g], pair, g, bd)
        for origin in sources:
            unpack(rbuf.at[origin, g], origin, g, bd)

        def keep(il):
            i = g * plan.rc + il
            for j in range(BLOCK_COLS):
                xt[i * BLOCK_COLS + j] = bd[r * plan.rows + i, :, j * t : (j + 1) * t]
        loop(plan.rc, keep)
    for g in range(chunks):
        take_relayed(rbuf, g, rrecv, relay_send)
        for origin in relayed:
            unpack(rbuf.at[origin, g], origin, g, bd)
    for g in range(chunks):
        multiply(pk.at[g], c, g, bd, acc, True)

    s_keys = slot_keys(plan, si_ref)

    def send_square(g):
        mine = s_keys[g * plan.pc : (g + 1) * plan.pc]
        for p, (_, key) in enumerate(mine):
            sk[g, p * t : (p + 1) * t, :] = acc[jnp.where(key < 0, plan.places, key)].astype(BF16)
        sk[g, plan.pc * t : plan.ch, :] = meta_of(plan, [key for _, key in mine])
        send_row(sk, sbuf, g, spair_send, scross_send, srecv)

    for g in range(chunks):
        multiply_pair(1, g, bd, acc)

    if plan.small:
        for d in range(2, n_col):
            for g in range(chunks):
                forward(d, g)
                multiply_pair(d, g, bd, acc)
                if d == n_col - 1:
                    send_square(g)
        if n_col == 2:
            for g in range(chunks):
                send_square(g)
    else:
        def later(d):
            for g in range(chunks):
                forward(d, g)
                multiply_pair(d, g, bd, acc)
        lax.fori_loop(2, n_col, lambda d, _: (later(d), 0)[1], 0)
        for g in range(chunks):
            send_square(g)

    for s, key in enumerate(out_keys(plan, si_ref)):
        sq_ref[0, 0, s] = acc[key].astype(BF16)

    for g in range(chunks):
        unpack(sk.at[g], r, g, sd)
        take_pair(sbuf, g, srecv, srelay_send)
        unpack(sbuf.at[pair, g], pair, g, sd)
        take_cross(sbuf, g, srelay_send, srecv)
        for origin in sources:
            unpack(sbuf.at[origin, g], origin, g, sd)
    for g in range(chunks):
        take_relayed(sbuf, g, srecv, srelay_send)
        for origin in relayed:
            unpack(sbuf.at[origin, g], origin, g, sd)

    if plan.small:
        for kb in range(n_col):
            left = ld[kb].reshape(plan.rows * t, plan.width)
            product = jnp.dot(left, right_of(sd, kb), preferred_element_type=F32)
            for i in range(plan.rows):
                add(acc2, i, product[i * t : (i + 1) * t], kb == 0)
    else:
        for g in range(chunks):
            multiply(pk.at[g], c, g, sd, acc2, True)

            def again(d):
                multiply_pair(d, g, sd, acc2)
            lax.fori_loop(1, n_col, lambda d, _: (again(d), 0)[1], 0)

    for s, key in enumerate(out_keys(plan, ni_ref)):
        rf_ref[0, 0, s] = (1.5 * xt[key].astype(F32) - 0.5 * acc2[key]).astype(BF16)

    for g in range(chunks):
        end_row(pk, rbuf, g, pair_send, cross_send, relay_send, rrecv)
        end_row(sk, sbuf, g, spair_send, scross_send, srelay_send, srecv)

        @pl.when(c < n_col - 1)
        def _():
            col_copy(pk.at[g], c, g, up_send, c + 1).wait_send()

        @pl.when(c > 0)
        def _():
            col_copy(pk.at[g], c, g, dn_send, c - 1).wait_send()

        def sent(d):
            @pl.when(jnp.logical_and(c >= d, c < n_col - 1))
            def _():
                col_copy(zbuf.at[c - d, g], c - d, g, up_send, c + 1).wait_send()

            @pl.when(jnp.logical_and(c + d < n_col, c > 0))
            def _():
                col_copy(zbuf.at[c + d, g], c + d, g, dn_send, c - 1).wait_send()
        if plan.small:
            for d in range(1, n_col):
                sent(d)
        else:
            lax.fori_loop(1, n_col, lambda d, _: (sent(d), 0)[1], 0)


CHUNKS = 2


def solution(mesh):
    n_col, n_row = mesh.shape["col"], mesh.shape["row"]

    def shards(x_tiles, x_index, square_index, new_index):
        slots, t = x_tiles.shape[2], x_tiles.shape[3]
        plan = Plan(n_col, n_row, slots, t, CHUNKS)
        k, ch, g = plan.rows * n_row, plan.ch, plan.chunks
        half = max(n_row // 2 - 1, 1)
        scratch = [
            pltpu.VMEM((g, ch, t), BF16),
            pltpu.VMEM((g, ch, t), BF16),
            pltpu.VMEM((n_col, g, ch, t), BF16),
            pltpu.VMEM((n_row, g, ch, t), BF16),
            pltpu.VMEM((n_row, g, ch, t), BF16),
            pltpu.VMEM((k, t, plan.width), BF16),
            pltpu.VMEM((n_col, plan.rows, t, plan.width) if plan.small else (1, 1, 16, t), BF16),
            pltpu.VMEM((plan.places + 1, t, t), F32),
            pltpu.VMEM((plan.places + 1, t, t), BF16),
        ]
        if plan.small:
            scratch += [
                pltpu.VMEM((k, t, plan.width), BF16),
                pltpu.VMEM((plan.places + 1, t, t), F32),
            ]
        dma = pltpu.SemaphoreType.DMA
        scratch += [dma((n_col, g))] * 3
        scratch += [dma((n_row, g)), dma((g,)), dma((half, g)), dma((half, g))] * 2
        shape = jax.ShapeDtypeStruct(x_tiles.shape, BF16)
        vmem = pl.BlockSpec(memory_space=pltpu.VMEM)
        smem = pl.BlockSpec(memory_space=pltpu.SMEM)
        return pl.pallas_call(
            functools.partial(kernel, plan),
            out_shape=(shape, shape),
            in_specs=[vmem, smem, smem, smem],
            out_specs=(vmem, vmem),
            scratch_shapes=scratch,
            compiler_params=pltpu.CompilerParams(
                collective_id=0, has_side_effects=True,
                vmem_limit_bytes=(24 if plan.small else 56) * 2**20,
            ),
        )(x_tiles, x_index, square_index, new_index)

    tiles = P(("parts", "row"), "col", None, None, None)
    index = P(("parts", "row"), "col", None, None)
    return jax.shard_map(
        shards, mesh=mesh, in_specs=(tiles, index, index, index), out_specs=(tiles, tiles), check_vma=False,
    )
```

time: 120 us -> 36.7 us (0.31)
  the two profiles are of different devices: /device:TPU:0 before, /device:TPU:1 now
where the time goes in v1:
time: 36.7 us; the launch traced here: 36.5 us
  Pallas kernels  31.4 us (86%)
  local copies, waits for them, and re-layouts  4.39 us (12%)
  between operations  0.65 us (2%)
    pallas_call x1, Pallas kernels, shards(): pl.pallas_call(functools.partial(kernel, plan), out_shape=(shape, shape),...  31.4 us
    unnamed x10, local copies, waits for them, and re-layouts  4.39 us

profile of v1, /device:TPU:1, one launch (start us, length us, event | category | flops | bytes accessed | tf_op | source)
XLA Modules:
  0.0 36.5 jit_solution(64762676826696183)
XLA Ops:
  0.6 0.0 copy-start
  0.6 0.9 %copy-done = bf16[1,1,8,128,128]{4,3,2,1,0:T(8,128)(2,1)S(1)} copy-done((bf16[1,1,8,128,128]{4,3,2,1,0:T(8,128)(2,1)S(1)}, bf16[1,1,8,128,128]{4,3,2,1,0:T(8,128)(2,1)}, u32[]{:S(2)}) %copy-start) | copy-done | bytes 262168
  1.6 0.0 copy-start.1
  1.6 0.7 %copy-done.1 = s32[1,1,2,8]{3,2,1,0:T(2,128)S(1)} copy-done((s32[1,1,2,8]{3,2,1,0:T(2,128)S(1)}, s32[1,1,2,8]{3,2,1,0:T(2,128)}, u32[]{:S(2)}) %copy-start.1) | copy-done | bytes 88
  2.3 0.0 copy-start.2
  2.3 0.7 %copy-done.2 = s32[1,1,2,8]{3,2,1,0:T(2,128)S(1)} copy-done((s32[1,1,2,8]{3,2,1,0:T(2,128)S(1)}, s32[1,1,2,8]{3,2,1,0:T(2,128)}, u32[]{:S(2)}) %copy-start.2) | copy-done | bytes 88
  2.9 0.0 copy-start.3
  2.9 0.7 %copy-done.3 = s32[1,1,2,8]{3,2,1,0:T(2,128)S(1)} copy-done((s32[1,1,2,8]{3,2,1,0:T(2,128)S(1)}, s32[1,1,2,8]{3,2,1,0:T(2,128)}, u32[]{:S(2)}) %copy-start.3) | copy-done | bytes 88
  3.6 31.4 %shard_map.59 = (bf16[1,1,8,128,128]{4,3,2,1,0:T(8,128)(2,1)S(1)}, bf16[1,1,8,128,128]{4,3,2,1,0:T(8,128)(2,1)S(1)}) custom-call(bf16[1,1,8,128,128]{4,3,2,1,0:T(8,128)(2,1)S(1)} %copy-done, s32[1,1,2,8]{3,2,1,0:T(2,128)S(1)} %copy-done.1, s32[1,1,2,8]{3,2,1,0:T(2,128)S(1)} %copy-done.2, s32[1,1,2,8]{3,2,1,0:T(2,128)S(1)} %copy-done.3), custom_call_target="tpu_custom_call" | custom-call | tf_op jit(solution)/shard_map/pallas_call | solution.py:398
  35.1 0.7 %copy.8 = bf16[1,1,8,128,128]{4,3,2,1,0:T(8,128)(2,1)} copy(bf16[1,1,8,128,128]{4,3,2,1,0:T(8,128)(2,1)S(1)} %get-tuple-element.4) | data formatting | bytes 524288
  35.8 0.7 %copy.9 = bf16[1,1,8,128,128]{4,3,2,1,0:T(8,128)(2,1)} copy(bf16[1,1,8,128,128]{4,3,2,1,0:T(8,128)(2,1)S(1)} %get-tuple-element.5) | data formatting | bytes 524288
Async XLA Ops:
  0.6 1.0 %copy-start = (bf16[1,1,8,128,128]{4,3,2,1,0:T(8,128)(2,1)S(1)}, bf16[1,1,8,128,128]{4,3,2,1,0:T(8,128)(2,1)}, u32[]{:S(2)}) copy-start(bf16[1,1,8,128,128]{4,3,2,1,0:T(8,128)(2,1)} %x_ref.1) | copy-start | bytes 786436
  1.6 0.7 %copy-start.1 = (s32[1,1,2,8]{3,2,1,0:T(2,128)S(1)}, s32[1,1,2,8]{3,2,1,0:T(2,128)}, u32[]{:S(2)}) copy-start(s32[1,1,2,8]{3,2,1,0:T(2,128)} %xi_ref.1) | copy-start | bytes 196
  2.3 0.7 %copy-start.2 = (s32[1,1,2,8]{3,2,1,0:T(2,128)S(1)}, s32[1,1,2,8]{3,2,1,0:T(2,128)}, u32[]{:S(2)}) copy-start(s32[1,1,2,8]{3,2,1,0:T(2,128)} %si_ref.1) | copy-start | bytes 196
  2.9 0.7 %copy-start.3 = (s32[1,1,2,8]{3,2,1,0:T(2,128)S(1)}, s32[1,1,2,8]{3,2,1,0:T(2,128)}, u32[]{:S(2)}) copy-start(s32[1,1,2,8]{3,2,1,0:T(2,128)} %ni_ref.1) | copy-start | bytes 196

commit v2 on v1

--- a/solution.py
+++ b/solution.py
@@ -35,7 +35,7 @@
         self.pc = self.pos // self.chunks
         self.ch = self.pc * tile + META
         self.places = self.rows * BLOCK_COLS
-        self.small = self.rows <= FEW and n_col <= FEW
+        self.small = self.canonical and self.rows == BLOCK_COLS and n_col <= FEW
         self.width = BLOCK_COLS * tile
         assert self.pc <= META and self.places <= 256 and n_row % 2 == 0
 
@@ -96,8 +96,9 @@
 
 def kernel(
     plan,
-    x_ref, xi_ref, si_ref, ni_ref,
+    x_in, xi_in, si_in, ni_in,
     sq_ref, rf_ref,
+    x_ref, xi_ref, si_ref, ni_ref, local_sem,
     pk, sk, zbuf, rbuf, sbuf, bd, ld, acc, xt, *rest,
 ):
     if plan.small:
@@ -114,6 +115,12 @@
     sources = [lax.rem(r + n_row - 2 * m, n_row) for m in hops]
     relayed = [lax.rem(pair + n_row - 2 * m, n_row) for m in hops]
 
+    takes = [
+        pltpu.make_async_copy(src, dst, local_sem.at[n])
+        for n, (src, dst) in enumerate(((xi_in, xi_ref), (x_in, x_ref), (si_in, si_ref), (ni_in, ni_ref)))
+    ]
+    for take in takes:
+        take.start()
     barrier = pltpu.get_barrier_semaphore()
 
     @pl.when(c > 0)
@@ -127,7 +134,9 @@
     for other in [pair] + crosses:
         pl.semaphore_signal(barrier, inc=1, device_id={"row": other}, device_id_type=MESH)
 
+    takes[0].wait()
     x_keys = slot_keys(plan, xi_ref)
+    takes[1].wait()
     for g in range(chunks):
         mine = x_keys[g * plan.pc : (g + 1) * plan.pc]
         for p, (slot, _) in enumerate(mine):
@@ -235,8 +244,15 @@
             return
         for il in range(plan.rc):
             for j, tile in enumerate(row_tiles(plan, chunk, g * plan.rc + il, il)):
-                ld[kb, g * plan.rc + il, :, j * t : (j + 1) * t] = tile
-        left = ld[kb, g * plan.rc : (g + 1) * plan.rc].reshape(plan.rc * t, plan.width)
+                part, at = divmod(j, plan.rc)
+                ld[part, kb, g * plan.rc + il, :, at * t : (at + 1) * t] = tile
+        left = jnp.concatenate(
+            [
+                ld[part, kb, g * plan.rc : (g + 1) * plan.rc].reshape(plan.rc * t, plan.rc * t)
+                for part in range(chunks)
+            ],
+            axis=1,
+        )
         product = jnp.dot(left, right_of(dense, kb), preferred_element_type=F32)
         for il in range(plan.rc):
             add(into, g * plan.rc + il, product[il * t : (il + 1) * t], first)
@@ -272,6 +288,8 @@
     for g in range(chunks):
         multiply(pk.at[g], c, g, bd, acc, True)
 
+    takes[2].wait()
+    takes[3].wait()
     s_keys = slot_keys(plan, si_ref)
 
     def send_square(g):
@@ -306,24 +324,43 @@
     for s, key in enumerate(out_keys(plan, si_ref)):
         sq_ref[0, 0, s] = acc[key].astype(BF16)
 
-    for g in range(chunks):
+    def add_square(g):
+        left = jnp.concatenate(
+            [ld[g, kb].reshape(plan.rows * t, plan.rc * t) for kb in range(n_col)], axis=1
+        )
+        right = jnp.concatenate(
+            [
+                sd[kb * plan.rows + g * plan.rc : kb * plan.rows + (g + 1) * plan.rc].reshape(
+                    plan.rc * t, plan.width
+                )
+                for kb in range(n_col)
+            ],
+            axis=0,
+        )
+        product = jnp.dot(left, right, preferred_element_type=F32)
+        for i in range(plan.rows):
+            add(acc2, i, product[i * t : (i + 1) * t], g == 0)
+
+    def take_square(g):
         unpack(sk.at[g], r, g, sd)
         take_pair(sbuf, g, srecv, srelay_send)
         unpack(sbuf.at[pair, g], pair, g, sd)
-        take_cross(sbuf, g, srelay_send, srecv)
         for origin in sources:
             unpack(sbuf.at[origin, g], origin, g, sd)
-    for g in range(chunks):
         take_relayed(sbuf, g, srecv, srelay_send)
         for origin in relayed:
             unpack(sbuf.at[origin, g], origin, g, sd)
 
+    for g in range(chunks - 1):
+        take_cross(sbuf, g, srelay_send, srecv)
+    for g in range(chunks - 1):
+        take_square(g)
+        if plan.small:
+            add_square(g)
+    take_cross(sbuf, chunks - 1, srelay_send, srecv)
+    take_square(chunks - 1)
     if plan.small:
-        for kb in range(n_col):
-            left = ld[kb].reshape(plan.rows * t, plan.width)
-            product = jnp.dot(left, right_of(sd, kb), preferred_element_type=F32)
-            for i in range(plan.rows):
-                add(acc2, i, product[i * t : (i + 1) * t], kb == 0)
+        add_square(chunks - 1)
     else:
         for g in range(chunks):
             multiply(pk.at[g], c, g, sd, acc2, True)
@@ -362,7 +399,7 @@
             lax.fori_loop(1, n_col, lambda d, _: (sent(d), 0)[1], 0)
 
 
-CHUNKS = 2
+CHUNKS = 4
 
 
 def solution(mesh):
@@ -374,13 +411,18 @@
         k, ch, g = plan.rows * n_row, plan.ch, plan.chunks
         half = max(n_row // 2 - 1, 1)
         scratch = [
+            pltpu.VMEM(x_tiles.shape, BF16),
+            pltpu.SMEM(x_index.shape, jnp.int32),
+            pltpu.SMEM(x_index.shape, jnp.int32),
+            pltpu.SMEM(x_index.shape, jnp.int32),
+            pltpu.SemaphoreType.DMA((6,)),
             pltpu.VMEM((g, ch, t), BF16),
             pltpu.VMEM((g, ch, t), BF16),
             pltpu.VMEM((n_col, g, ch, t), BF16),
             pltpu.VMEM((n_row, g, ch, t), BF16),
             pltpu.VMEM((n_row, g, ch, t), BF16),
             pltpu.VMEM((k, t, plan.width), BF16),
-            pltpu.VMEM((n_col, plan.rows, t, plan.width) if plan.small else (1, 1, 16, t), BF16),
+            pltpu.VMEM((g, n_col, plan.rows, t, plan.rc * t) if plan.small else (1, 1, 1, 16, t), BF16),
             pltpu.VMEM((plan.places + 1, t, t), F32),
             pltpu.VMEM((plan.places + 1, t, t), BF16),
         ]
@@ -393,17 +435,17 @@
         scratch += [dma((n_col, g))] * 3
         scratch += [dma((n_row, g)), dma((g,)), dma((half, g)), dma((half, g))] * 2
         shape = jax.ShapeDtypeStruct(x_tiles.shape, BF16)
-        vmem = pl.BlockSpec(memory_space=pltpu.VMEM)
-        smem = pl.BlockSpec(memory_space=pltpu.SMEM)
+        whole = pl.BlockSpec(memory_space=pltpu.HBM)
+        there = pl.BlockSpec(memory_space=pltpu.VMEM)
         return pl.pallas_call(
             functools.partial(kernel, plan),
             out_shape=(shape, shape),
-            in_specs=[vmem, smem, smem, smem],
-            out_specs=(vmem, vmem),
+            in_specs=[whole] * 4,
+            out_specs=(there, there),
             scratch_shapes=scratch,
             compiler_params=pltpu.CompilerParams(
                 collective_id=0, has_side_effects=True,
-                vmem_limit_bytes=(24 if plan.small else 56) * 2**20,
+                vmem_limit_bytes=(62 if plan.small else 56) * 2**20,
             ),
         )(x_tiles, x_index, square_index, new_index)
 

time: 36.7 us -> 34.3 us (0.935)
  the two profiles are of different devices: /device:TPU:1 before, /device:TPU:0 now
where the time goes in v2:
time: 34.3 us; the launch traced here: 34.2 us
  Pallas kernels  31.1 us (91%)
  local copies, waits for them, and re-layouts  2.42 us (7%)
  between operations  0.65 us (2%)
    pallas_call x1, Pallas kernels, shards(): pl.pallas_call(functools.partial(kernel, plan), out_shape=(shape, shape),...  31.1 us
    unnamed x4, local copies, waits for them, and re-layouts  2.42 us

profile of v2, /device:TPU:0, one launch (start us, length us, event | category | flops | bytes accessed | tf_op | source)
XLA Modules:
  0.0 34.2 jit_solution(12075973468322333106)
XLA Ops:
  0.6 31.1 %shard_map.59 = (bf16[1,1,8,128,128]{4,3,2,1,0:T(8,128)(2,1)}, bf16[1,1,8,128,128]{4,3,2,1,0:T(8,128)(2,1)}) custom-call(bf16[1,1,8,128,128]{4,3,2,1,0:T(8,128)(2,1)} %x_in.1, s32[1,1,2,8]{3,2,1,0:T(2,128)} %xi_in.1, s32[1,1,2,8]{3,2,1,0:T(2,128)} %si_in.1, s32[1,1,2,8]{3,2,1,0:T(2,128)} %ni_in.1), custom_call_target="tpu_custom_call" | custom-call | tf_op jit(solution)/shard_map/pallas_call | solution.py:440
  31.7 0.0 copy-start
  31.7 1.7 %copy.8 = bf16[1,1,8,128,128]{4,3,2,1,0:T(8,128)(2,1)} copy(bf16[1,1,8,128,128]{4,3,2,1,0:T(8,128)(2,1)} %get-tuple-element.4) | data formatting | bytes 524288
  33.5 0.0 copy-done
  33.5 0.7 %copy.9 = bf16[1,1,8,128,128]{4,3,2,1,0:T(8,128)(2,1)} copy(bf16[1,1,8,128,128]{4,3,2,1,0:T(8,128)(2,1)S(1)} %copy-done) | data formatting | bytes 524288
Async XLA Ops:
  31.7 1.7 %copy-start = (bf16[1,1,8,128,128]{4,3,2,1,0:T(8,128)(2,1)S(1)}, bf16[1,1,8,128,128]{4,3,2,1,0:T(8,128)(2,1)}, u32[]{:S(2)}) copy-start(bf16[1,1,8,128,128]{4,3,2,1,0:T(8,128)(2,1)} %get-tuple-element.5) | copy-start | bytes 786436

commit v3 on v2

--- a/solution.py
+++ b/solution.py
@@ -192,6 +192,7 @@
         def _():
             col_copy(pk.at[g], c, g, dn_send, c - 1).start()
 
+    for g in range(chunks):
         send_row(pk, rbuf, g, pair_send, cross_send, rrecv)
 
     acc[plan.places] = jnp.zeros((t, t), F32)

time: 34.3 us -> 34.3 us (level)
  no operation moved by 1% of the time
where the time goes in v3:
time: 34.3 us; the launch traced here: 34.2 us
  Pallas kernels  31.1 us (91%)
  local copies, waits for them, and re-layouts  2.42 us (7%)
  between operations  0.65 us (2%)
    pallas_call x1, Pallas kernels, shards(): pl.pallas_call(functools.partial(kernel, plan), out_shape=(shape, shape),...  31.1 us
    unnamed x4, local copies, waits for them, and re-layouts  2.42 us

profile of v3, /device:TPU:0, one launch (start us, length us, event | category | flops | bytes accessed | tf_op | source)
XLA Modules:
  0.0 34.2 jit_solution(16728748771766462621)
XLA Ops:
  0.6 31.1 %shard_map.59 = (bf16[1,1,8,128,128]{4,3,2,1,0:T(8,128)(2,1)}, bf16[1,1,8,128,128]{4,3,2,1,0:T(8,128)(2,1)}) custom-call(bf16[1,1,8,128,128]{4,3,2,1,0:T(8,128)(2,1)} %x_in.1, s32[1,1,2,8]{3,2,1,0:T(2,128)} %xi_in.1, s32[1,1,2,8]{3,2,1,0:T(2,128)} %si_in.1, s32[1,1,2,8]{3,2,1,0:T(2,128)} %ni_in.1), custom_call_target="tpu_custom_call" | custom-call | tf_op jit(solution)/shard_map/pallas_call | solution.py:441
  31.7 0.0 copy-start
  31.7 1.7 %copy.8 = bf16[1,1,8,128,128]{4,3,2,1,0:T(8,128)(2,1)} copy(bf16[1,1,8,128,128]{4,3,2,1,0:T(8,128)(2,1)} %get-tuple-element.4) | data formatting | bytes 524288
  33.5 0.0 copy-done
  33.5 0.7 %copy.9 = bf16[1,1,8,128,128]{4,3,2,1,0:T(8,128)(2,1)} copy(bf16[1,1,8,128,128]{4,3,2,1,0:T(8,128)(2,1)S(1)} %copy-done) | data formatting | bytes 524288
Async XLA Ops:
  31.7 1.7 %copy-start = (bf16[1,1,8,128,128]{4,3,2,1,0:T(8,128)(2,1)S(1)}, bf16[1,1,8,128,128]{4,3,2,1,0:T(8,128)(2,1)}, u32[]{:S(2)}) copy-start(bf16[1,1,8,128,128]{4,3,2,1,0:T(8,128)(2,1)} %get-tuple-element.5) | copy-start | bytes 786436
